TPU v7x, 32 devices: a whole 2x2x4 slice. The times are simulated.
32 devices in a mesh: aux: 4 (over y, core), virt: 8 (over z, x).
Axes of the slice: x: 2, y: 2, z: 4, core: 2. Of those that a mesh axis runs over, the one named last changes fastest.
Arguments:
- row_codes: bfloat16 [4, 128, 1920], P('aux'), may hold values from -4 to 4
- row_scales: float32 [4, 128, 15], P('aux'), may hold values from 0.2 to 2
- panel_codes: bfloat16 [4, 1920, 1920], P('aux', 'virt'), may hold values from -4 to 4
- panel_scales: float32 [4, 1920, 15], P('aux', 'virt'), may hold values from 0.0034232659 to 0.03423266
- amplitudes: bfloat16 [16, 1920, 1920], P('aux', 'virt'), may hold values from -0.125 to 0.125
Outputs:
- residual: float32 [1920, 16, 128], P('virt', 'aux')
All inputs are finite; a program needn't handle non-finite values.
Results may differ from a plain program's by a relative error of at most 0.005.
Values may be sent and summed in bfloat16 or wider, within the bound.
A program may use at most 128 MiB of HBM per device.

v0:
```python
import jax
import jax.numpy as jnp
from jax import lax
from jax.sharding import PartitionSpec as P


def decode_rows(codes, scales):
    count, width, length = codes.shape
    blocks = scales.shape[2]
    wide = (
        codes.astype(jnp.float32).reshape(count, width, blocks, length // blocks)
        * scales[:, :, :, None]
    )
    return wide.reshape(count, width, length).astype(jnp.bfloat16)


def on_device(row_codes, row_scales, panel_codes, panel_scales, amplitudes):
    row_local = decode_rows(row_codes, row_scales)
    panel_local = decode_rows(panel_codes, panel_scales)
    row_all = lax.all_gather(row_local, "aux", axis=0, tiled=True)
    half = jnp.einsum(
        "qac,pdc->pqda", row_all, amplitudes, preferred_element_type=jnp.float32
    ).astype(jnp.bfloat16)
    total = jnp.einsum(
        "qdb,pqda->bpa",
        lax.all_gather(panel_local, "aux", axis=0, tiled=True),
        half,
        preferred_element_type=jnp.float32,
    )
    return lax.psum_scatter(total, "virt", scatter_dimension=0, tiled=True)


def solution(mesh):
    placed = (
        P("aux", None, None),
        P("aux", None, None),
        P("aux", "virt", None),
        P("aux", "virt", None),
        P("aux", "virt", None),
    )
    return jax.shard_map(
        on_device, mesh=mesh, in_specs=placed, out_specs=P("virt", "aux", None), check_vma=False
    )
```

profile of v0, /device:TPU:0, one launch (start us, length us, event | category | flops | bytes accessed | tf_op | source)
XLA Modules:
  0.0 170.6 jit_solution(15583074885885220916)
XLA Ops:
  6.5 0.0 all-gather.5.cloned.1.call-start
  6.5 0.7 copy.21
  7.2 1.3 copy.13
  8.5 0.1 fusion.18
  8.6 0.0 copy-start
  8.7 1.0 copy.14
  9.7 0.0 all-gather.5.cloned.1.call-update
  9.7 0.0 all-gather.3.cloned.1.call-start
  9.7 0.8 copy.18
  10.6 0.6 mul.33
  11.1 1.5 mul.34
  12.6 0.0 copy-done
  12.6 2.6 %multiply_convert_fusion = bf16[1,240,1920]{2,1,0:T(8,128)(2,1)} fusion(f32[1,240,1920]{2,1,0:T(8,128)} %mul.34, bf16[1,240,1920]{2,1,0:T(8,128)(2,1)S(1)} %copy-done), kind=kLoop, calls=%fused_computation.6 | loop fusion | flops 1382400 | bytes 3686400 | tf_op jit(solution)/shard_map/convert_element_type | solution.py:14
  15.3 0.0 all-gather.3.cloned.1.call-update
  15.3 0.0 reduce-scatter.2.cloned.1.call-start
  15.3 19.0 %all-gather.5.cloned.1.call-done = bf16[4,128,1920]{2,1,0:T(8,128)(2,1)} async-done(((bf16[1,128,1920]{2,1,0:T(8,128)(2,1)}), bf16[4,128,1920]{2,1,0:T(8,128)(2,1)}) %all-gather.5.cloned.1.call-update) | async-done | bytes 1966096 | tf_op jit(solution)/shard_map/all_gather | solution.py:20
  34.4 33.2 %all-gather.3.cloned.1.call-done = bf16[4,240,1920]{2,1,0:T(8,128)(2,1)} async-done(((bf16[1,240,1920]{2,1,0:T(8,128)(2,1)}), bf16[4,240,1920]{2,1,0:T(8,128)(2,1)}) %all-gather.3.cloned.1.call-update) | async-done | bytes 3686416 | tf_op jit(solution)/shard_map/all_gather | solution.py:26
  67.6 10.0 %fusion.4 = f32[1920,4,128]{2,0,1:T(8,128)} fusion(bf16[4,240,1920]{2,1,0:T(8,128)(2,1)} %all-gather.3.cloned.1.call-done, bf16[4,240,1920]{2,1,0:T(8,128)(2,1)} %param.9, bf16[4,128,1920]{2,1,0:T(8,128)(2,1)} %all-gather.5.cloned.1.call-done), kind=kOutput, calls=%fused_computation.4 | convolution fusion | flops 3775365120 | bytes 13271040 | tf_op jit(solution)/shard_map/qdb,pqda->bpa/dot_general | solution.py:24
  77.6 0.0 reduce-scatter.2.cloned.1.call-update
  77.6 84.5 %reduce-scatter.2.cloned.1.call-done = f32[240,4,128]{2,0,1:T(8,128)} async-done(((f32[1920,4,128]{2,0,1:T(8,128)}), f32[240,4,128]{2,0,1:T(8,128)}) %reduce-scatter.2.cloned.1.call-update) | async-done | bytes 491536 | tf_op jit(solution)/shard_map/reduce_scatter | solution.py:30
  162.1 2.0 %copy.15 = f32[240,4,128]{2,1,0:T(4,128)} copy(f32[240,4,128]{2,0,1:T(8,128)} %reduce-scatter.2.cloned.1.call-done) | data formatting | bytes 983040 | tf_op jit(solution)/shard_map/reduce_scatter | solution.py:30
Async XLA Ops:
  6.5 27.9 %all-gather.5.cloned.1.call-start = ((), (), s32[]{:S(2)}) async-start(), calls=%async_computation.2 | async-start | bytes 2457600 | tf_op jit(solution)/shard_map/all_gather | solution.py:20
  8.6 4.0 %copy-start = (bf16[1,240,1920]{2,1,0:T(8,128)(2,1)S(1)}, bf16[1,240,1920]{2,1,0:T(8,128)(2,1)}, u32[]{:S(2)}) copy-start(bf16[1,240,1920]{2,1,0:T(8,128)(2,1)} %param.7) | copy-start | bytes 2764804
  9.7 57.9 %all-gather.3.cloned.1.call-start = ((), (), s32[]{:S(2)}) async-start(), calls=%async_computation.1 | async-start | bytes 4608000 | tf_op jit(solution)/shard_map/all_gather | solution.py:26
  15.3 146.8 %reduce-scatter.2.cloned.1.call-start = ((), (), s32[]{:S(2)}) async-start(), calls=%async_computation.3 | async-start | bytes 4423680 | tf_op jit(solution)/shard_map/reduce_scatter | solution.py:30
Sparse Core Ops, SparseCore 0:
  9.8 24.5 all-gather.4
  35.9 31.5 all-gather.2
  77.7 84.3 reduce-scatter.1
where the time goes:
time: 171 us
  waiting for transfers between devices  137 us (80%)
  between operations  13.1 us (8%)
  matrix products  9.98 us (6%)
  local copies, waits for them, and re-layouts  7.91 us (5%)
  other arithmetic  2.72 us (2%)
    reduce_scatter x1, waiting for transfers between devices, on_device(): return lax.psum_scatter(total, 'virt', scatter_dimension=0, tiled=True)  84.5 us
    all_gather x1, waiting for transfers between devices, on_device(): lax.all_gather(panel_local, 'aux', axis=0, tiled=True)  33.2 us
    all_gather x1, waiting for transfers between devices, on_device(): row_all = lax.all_gather(row_local, 'aux', axis=0, tiled=True)  19 us
    dot_general x1, matrix products, on_device(): jnp.einsum('qdb,pqda->bpa', lax.all_gather(panel_local, 'aux', axis=0, ti...  9.98 us
  transfers between devices with their start and end apart: 3, of which 3 were waited for; matrix products, arithmetic and copies ran while one was open for 3% of the time, Pallas kernels for 0%

commit v1 on v0

v1 whole, which is shorter than its diff:
```python
import functools

import jax
import jax.numpy as jnp
from jax import lax
from jax.experimental import pallas as pl
from jax.experimental.pallas import tpu as pltpu
from jax.sharding import PartitionSpec as P

MESH = pl.DeviceIdType.MESH
BF16 = jnp.bfloat16
F32 = jnp.float32


def kernel(
    na, nhi, nlo,
    rowc, rows_, panc, pans, amp_hbm, out,
    rowbuf, pg, half, amp, own, xs, xr, zs, zr,
    amp_sem, row0, ry, rx, rm, pm, py, pf, xsem, zsem,
):
    npair, d, length = amp.shape
    width = rowc.shape[1]
    blocks = rows_.shape[2]
    blk = length // blocks
    dp = pg.shape[3]
    bw = pg.shape[2]
    ny = na // 2
    nw = nhi * nlo
    part = width // nlo

    i = lax.axis_index("aux")
    j = lax.axis_index("virt")
    chip, core = i // 2, i % 2
    hi, lo = j // nlo, j % nlo
    mate_i = chip * 2 + (1 - core)

    def chip_at(o):
        return lax.rem(chip + o + ny, ny)

    def lo_at(s):
        return lax.rem(lo + s + nlo, nlo)

    def hi_at(t):
        return lax.rem(hi + t + nhi, nhi)

    mate = (mate_i, j)

    def over(o):
        return (chip_at(o) * 2 + core, j)

    def beside(s):
        return (i, hi * nlo + lo_at(s))

    def along(t):
        return (i, hi_at(t) * nlo + lo)

    amp_in = pltpu.make_async_copy(amp_hbm, amp, amp_sem)
    amp_in.start()

    barrier = pltpu.get_barrier_semaphore()
    partners = [mate] + [over(o) for o in range(1, ny)]
    partners += [beside(s) for s in range(1, nlo)] + [along(t) for t in range(1, nhi)]
    for who in partners:
        pl.semaphore_signal(barrier, inc=1, device_id=who, device_id_type=MESH)

    my_row = pl.multiple_of(i * width, width)
    for k in range(blocks):
        at = slice(k * blk, (k + 1) * blk)
        rowbuf[pl.ds(my_row, width), at] = (
            rowc[0, :, at].astype(F32) * rows_[0, :, k : k + 1]
        ).astype(BF16)

    pl.semaphore_wait(barrier, len(partners))

    def send(ref, sems, who):
        return pltpu.make_async_remote_copy(
            src_ref=ref, dst_ref=ref, send_sem=sems[0], recv_sem=sems[1],
            device_id=who, device_id_type=MESH,
        )

    def piece(q, p):
        return rowbuf.at[pl.ds(pl.multiple_of(q * width + p * part, part), part)]

    def row_mate(q):
        ref = rowbuf.at[pl.ds(pl.multiple_of(q * width, width), width)]
        return send(ref, (row0.at[0], row0.at[1]), mate)

    def row_over(o, q):
        return send(piece(q, lo), (ry.at[0, o], ry.at[1, o]), over(o))

    def row_beside(o, s, p):
        q = chip_at(-o) * 2 + core
        return send(piece(q, p), (rx.at[0, o, s], rx.at[1, o, s]), beside(s))

    def row_fwd(o, s, c):
        q = chip_at(-o) * 2 + c
        return send(piece(q, lo_at(-s)), (rm.at[0, o, s], rm.at[1, o, s]), mate)

    row_mate(i).start()
    for o in range(1, ny):
        row_over(o, i).start()

    half[...] = jnp.zeros_like(half)
    for k in range(blocks):
        at = slice(k * blk, (k + 1) * blk)
        dec = panc[0, :, at].astype(F32) * pans[0, :, k : k + 1]
        if dp > d:
            dec = jnp.concatenate([dec, jnp.zeros((dp - d, blk), F32)], axis=0)
        turned = dec.T
        first = k * blk
        while first < (k + 1) * blk:
            c = first // bw
            last = min((c + 1) * bw, (k + 1) * blk)
            pg[i, c, first - c * bw : last - c * bw, :] = turned[
                first - k * blk : last - k * blk
            ].astype(BF16)
            first = last

    def block_of(t, s):
        return hi_at(t) * nlo + lo_at(s)

    def pan_mate(q, t, s):
        n = (t - 1) * nlo + (s - 1)
        return send(pg.at[q, block_of(t, s)], (pm.at[0, n], pm.at[1, n]), mate)

    def pan_over(o, q, t, s):
        n = (t - 1) * nlo + (s - 1)
        return send(pg.at[q, block_of(t, s)], (py.at[0, o, n], py.at[1, o, n]), over(o))

    def pan_fwd(o, c, t, s):
        n = (t - 1) * nlo + (s - 1)
        q = chip_at(-o) * 2 + c
        return send(pg.at[q, block_of(t, s)], (pf.at[0, o, n], pf.at[1, o, n]), mate)

    for t in range(1, nhi + 1):
        for s in range(1, nlo + 1):
            for o in range(1, ny):
                pan_over(o, i, t, s).start()
            pan_mate(i, t, s).start()

    def half_of(k):
        both = rowbuf[pl.ds(pl.multiple_of(k * 2 * width, 2 * width), 2 * width), :]

        for p in range(npair):
            got = lax.dot_general(
                amp[p], both, (((1,), (1,)), ((), ())), preferred_element_type=F32
            ).astype(BF16)
            for c in range(2):
                half[k * 2 + c, 0:d, p * width : (p + 1) * width] = got[
                    :, c * width : (c + 1) * width
                ]

    amp_in.wait()
    row_mate(mate_i).wait_recv()
    half_of(chip)

    for o in range(1, ny):
        q = chip_at(-o) * 2 + core
        row_over(o, q).wait_recv()
        for s in range(1, nlo):
            row_beside(o, s, lo).start()
        row_fwd(o, 0, core).start()
    for o in range(1, ny):
        for s in range(1, nlo):
            row_beside(o, s, lo_at(-s)).wait_recv()
            row_fwd(o, s, core).start()

    def half_far(o, carry):
        for s in range(nlo):
            row_fwd(o, s, 1 - core).wait_recv()
        half_of(chip_at(-o))
        return carry

    lax.fori_loop(1, ny, half_far, 0)

    def x_send(t, s):
        return pltpu.make_async_remote_copy(
            src_ref=xs.at[t - 1, s - 1], dst_ref=xr.at[t - 1, s - 1],
            send_sem=xsem.at[0, t - 1, s - 1], recv_sem=xsem.at[1, t - 1, s - 1],
            device_id=beside(s), device_id_type=MESH,
        )

    def z_send(t):
        return pltpu.make_async_remote_copy(
            src_ref=zs.at[t - 1], dst_ref=zr.at[t - 1],
            send_sem=zsem.at[0, t - 1], recv_sem=zsem.at[1, t - 1],
            device_id=along(t), device_id_type=MESH,
        )

    def dot(q, b):
        return jnp.dot(pg[q, b], half[q], preferred_element_type=F32)

    def added(t):
        total = own[t - 1]
        for s in range(1, nlo):
            x_send(t, s).wait_recv()
            total = total + xr[t - 1, s - 1].astype(F32)
        return total

    def pass_on(t):
        zs[t - 1] = added(t).astype(BF16)
        z_send(t).start()

    def step(t, carry):
        for s in range(1, nlo + 1):
            b = block_of(t, s)
            for o in range(1, ny):
                q = chip_at(-o) * 2 + core
                pan_over(o, q, t, s).wait_recv()
                pan_fwd(o, core, t, s).start()
            pan_mate(mate_i, t, s).wait_recv()
            acc = dot(i, b) + dot(mate_i, b)
            for o in range(1, ny):
                acc = acc + dot(chip_at(-o) * 2 + core, b)
            for o in range(1, ny):
                pan_fwd(o, 1 - core, t, s).wait_recv()
                acc = acc + dot(chip_at(-o) * 2 + 1 - core, b)
            if s < nlo:
                xs[t - 1, s - 1] = acc.astype(BF16)
                x_send(t, s).start()
            else:
                own[t - 1] = acc

        @pl.when(t > 1)
        def _():
            pass_on(t - 1)

        return carry

    lax.fori_loop(1, nhi + 1, step, 0)

    total = added(nhi)
    for t in range(1, nhi):
        z_send(t).wait_recv()
        total = total + zr[t - 1].astype(F32)
    for p in range(npair):
        out[:, p, :] = total[:, p * width : (p + 1) * width]

    row_mate(i).wait_send()
    for o in range(1, ny):
        row_over(o, i).wait_send()
        row_fwd(o, 0, core).wait_send()
        for s in range(1, nlo):
            row_beside(o, s, lo).wait_send()
            row_fwd(o, s, core).wait_send()

    def drain(t, carry):
        for s in range(1, nlo + 1):
            pan_mate(i, t, s).wait_send()
            for o in range(1, ny):
                pan_over(o, i, t, s).wait_send()
                pan_fwd(o, core, t, s).wait_send()
            if s < nlo:
                x_send(t, s).wait_send()
        return carry

    lax.fori_loop(1, nhi + 1, drain, 0)
    for t in range(1, nhi):
        z_send(t).wait_send()


def on_device(na, nhi, nlo, row_codes, row_scales, panel_codes, panel_scales, amplitudes):
    npair, d, length = amplitudes.shape
    width = row_codes.shape[1]
    nw = nhi * nlo
    bw = length // nw
    dp = -(-d // 128) * 128
    ny = na // 2
    cols = npair * width
    dma = pltpu.SemaphoreType.DMA
    vmem = pl.BlockSpec(memory_space=pltpu.VMEM)
    return pl.pallas_call(
        functools.partial(kernel, na, nhi, nlo),
        out_shape=jax.ShapeDtypeStruct((bw, npair, width), F32),
        in_specs=[vmem, vmem, vmem, vmem, pl.BlockSpec(memory_space=pl.ANY)],
        out_specs=vmem,
        scratch_shapes=[
            pltpu.VMEM((na * width, length), BF16),
            pltpu.VMEM((na, nw, bw, dp), BF16),
            pltpu.VMEM((na, dp, cols), BF16),
            pltpu.VMEM((npair, d, length), BF16),
            pltpu.VMEM((nhi, bw, cols), F32),
            pltpu.VMEM((nhi, nlo - 1, bw, cols), BF16),
            pltpu.VMEM((nhi, nlo - 1, bw, cols), BF16),
            pltpu.VMEM((nhi - 1, bw, cols), BF16),
            pltpu.VMEM((nhi - 1, bw, cols), BF16),
            dma(()),
            dma((2,)),
            dma((2, ny)),
            dma((2, ny, nlo)),
            dma((2, ny, nlo)),
            dma((2, nw)),
            dma((2, ny, nw)),
            dma((2, ny, nw)),
            dma((2, nhi, nlo - 1)),
            dma((2, nhi - 1)),
        ],
        compiler_params=pltpu.CompilerParams(
            collective_id=0, has_side_effects=True, vmem_limit_bytes=56 * 1024 * 1024
        ),
        cost_estimate=pl.CostEstimate(
            flops=4 * npair * d * length * na * width,
            bytes_accessed=2 * npair * d * length,
            transcendentals=0,
        ),
    )(row_codes, row_scales, panel_codes, panel_scales, amplitudes)


def solution(mesh):
    na, nw = mesh.shape["aux"], mesh.shape["virt"]
    nlo = 4 if nw % 16 == 0 else 2
    placed = (
        P("aux", None, None),
        P("aux", None, None),
        P("aux", "virt", None),
        P("aux", "virt", None),
        P("aux", "virt", None),
    )
    return jax.shard_map(
        functools.partial(on_device, na, nw // nlo, nlo),
        mesh=mesh, in_specs=placed, out_specs=P("virt", "aux", None), check_vma=False,
    )
```

time: 171 us -> 60.1 us (0.35)
  waiting for transfers between devices: 137 us -> 0 us
  Pallas kernels: 0 us -> 55.1 us
  between operations: 13.1 us -> 0.01 us
  matrix products: 9.98 us -> 0 us
  local copies, waits for them, and re-layouts: 7.91 us -> 4.72 us
  other arithmetic: 2.72 us -> 0 us
    reduce_scatter x1 -> x0, waiting for transfers between devices: 84.5 us -> none  [on_device(): return lax.psum_scatter(total, 'virt', scatter_dimension=0, tiled=True)]
    pallas_call x0 -> x1, Pallas kernels: none -> 55.1 us  [on_device(): pl.pallas_call(functools.partial(kernel, na, nhi, nlo), out_shape=jax.Sha...]
    all_gather x2 -> x0, waiting for transfers between devices: 52.2 us -> none  [the longest x1 33.2 us: on_device(): lax.all_gather(panel_local, 'aux', axis=0, tiled=True)]
    dot_general x1 -> x0, matrix products: 9.98 us -> none  [on_device(): jnp.einsum('qdb,pqda->bpa', lax.all_gather(panel_local, 'aux', axis=0, ti...]
    mul x3 -> x0, local copies, waits for them, and re-layouts: 2.92 us -> none  [decode_rows(): codes.astype(jnp.float32).reshape(count, width, blocks, length // blocks)]
    unnamed x4 -> x3, local copies, waits for them, and re-layouts: 2 us -> 4.72 us
    convert_element_type x2 -> x0, other arithmetic: 2.72 us -> none  [decode_rows(): return wide.reshape(count, width, length).astype(jnp.bfloat16)]
    reduce_scatter x1 -> x0, local copies, waits for them, and re-layouts: 2 us -> none  [on_device(): return lax.psum_scatter(total, 'virt', scatter_dimension=0, tiled=True)]
  transfers between devices with their start and end apart: 3 -> 0, of which waited for: 3 -> 0; matrix products, arithmetic and copies ran while one was open for 3% -> 0% of each run, Pallas kernels for 0% -> 0%
where the time goes in v1:
time: 60.1 us; the launch traced here: 59.8 us
  Pallas kernels  55.1 us (92%)
  local copies, waits for them, and re-layouts  4.72 us (8%)
    pallas_call x1, Pallas kernels, on_device(): pl.pallas_call(functools.partial(kernel, na, nhi, nlo), out_shape=jax.Sha...  55.1 us
    unnamed x3, local copies, waits for them, and re-layouts  4.72 us

profile of v1, /device:TPU:0, one launch (start us, length us, event | category | flops | bytes accessed | tf_op | source)
XLA Modules:
  0.0 59.8 jit_solution(3779698252273031670)
XLA Ops:
  0.0 1.4 %copy.6.rows_ = f32[1,128,15]{2,1,0:T(8,128)} copy(f32[1,128,15]{1,0,2:T(1,128)} %param.6) | data formatting | bytes 15360 | tf_op args[1]
  1.4 1.5 %copy.7.pans = f32[1,240,15]{2,1,0:T(8,128)} copy(f32[1,240,15]{1,0,2:T(1,128)} %param.8) | data formatting | bytes 28800 | tf_op args[3]
  2.9 55.1 %shard_map.55 = f32[240,4,128]{2,1,0:T(4,128)} custom-call(bf16[1,128,1920]{2,1,0:T(8,128)(2,1)} %rowc.1, f32[1,128,15]{2,1,0:T(8,128)} %copy.6.rows_, bf16[1,240,1920]{2,1,0:T(8,128)(2,1)} %panc.1, f32[1,240,15]{2,1,0:T(8,128)} %copy.7.pans, bf16[4,240,1920]{2,1,0:T(8,128)(2,1)} %amp_hbm.1), custom_call_target="tpu_custom_call" | custom-call | flops 3774873600 | bytes 3686400 | tf_op jit(solution)/shard_map/pallas_call | solution.py:272
  58.0 1.8 %copy.9 = f32[240,4,128]{2,1,0:T(4,128)} copy(f32[240,4,128]{2,1,0:T(4,128)} %shard_map.55) | data formatting | bytes 983040

commit v2 on v1

v2 whole, which is shorter than its diff:
```python
import functools

import jax
import jax.numpy as jnp
from jax import lax
from jax.experimental import pallas as pl
from jax.experimental.pallas import tpu as pltpu
from jax.sharding import PartitionSpec as P

MESH = pl.DeviceIdType.MESH
BF16 = jnp.bfloat16
F32 = jnp.float32


def kernel(
    na, nhi, nlo,
    rowc, rows_, panc, pans, amp_hbm, out,
    rowbuf, pg, half, amp, own, xs, xr, zs, zr,
    amp_sem, row0, ry, rx, rm, pm, py, pf, xsem, zsem,
):
    npair, d, length = amp.shape
    width = rowc.shape[1]
    blocks = rows_.shape[0]
    blk = length // blocks
    dp = pg.shape[3]
    bw = pg.shape[2]
    ny = na // 2
    nw = nhi * nlo
    part = width // nlo
    subs = part // 16
    cuts = own.shape[1]
    cw = own.shape[3]

    i = lax.axis_index("aux")
    j = lax.axis_index("virt")
    chip, core = i // 2, i % 2
    hi, lo = j // nlo, j % nlo
    mate_i = chip * 2 + (1 - core)

    def chip_at(o):
        return lax.rem(chip + o + ny, ny)

    def lo_at(s):
        return lax.rem(lo + s + nlo, nlo)

    def hi_at(t):
        return lax.rem(hi + t + nhi, nhi)

    mate = (mate_i, j)

    def over(o):
        return (chip_at(o) * 2 + core, j)

    def beside(s):
        return (i, hi * nlo + lo_at(s))

    def along(t):
        return (i, hi_at(t) * nlo + lo)

    amp_in = pltpu.make_async_copy(amp_hbm, amp, amp_sem)
    amp_in.start()

    barrier = pltpu.get_barrier_semaphore()
    partners = [mate] + [over(o) for o in range(1, ny)]
    partners += [beside(s) for s in range(1, nlo)] + [along(t) for t in range(1, nhi)]
    for who in partners:
        pl.semaphore_signal(barrier, inc=1, device_id=who, device_id_type=MESH)

    by_row = rows_[:, 0, :].T
    my_row = pl.multiple_of(i * width, width)
    for k in range(blocks):
        at = slice(k * blk, (k + 1) * blk)
        rowbuf[pl.ds(my_row, width), at] = (
            rowc[0, :, at].astype(F32) * by_row[:, k : k + 1]
        ).astype(BF16)

    pl.semaphore_wait(barrier, len(partners))

    def send(ref, sems, who):
        return pltpu.make_async_remote_copy(
            src_ref=ref, dst_ref=ref, send_sem=sems[0], recv_sem=sems[1],
            device_id=who, device_id_type=MESH,
        )

    def piece(q, p, g):
        return rowbuf.at[pl.ds(pl.multiple_of(q * width + p * part + g * 16, 16), 16)]

    def row_mate(q):
        ref = rowbuf.at[pl.ds(pl.multiple_of(q * width, width), width)]
        return send(ref, (row0.at[0], row0.at[1]), mate)

    def row_over(o, q, g):
        return send(piece(q, lo, g), (ry.at[0, o, g], ry.at[1, o, g]), over(o))

    def row_beside(o, s, p, g):
        q = chip_at(-o) * 2 + core
        return send(piece(q, p, g), (rx.at[0, o, s, g], rx.at[1, o, s, g]), beside(s))

    def row_fwd(o, s, c, g):
        q = chip_at(-o) * 2 + c
        return send(piece(q, lo_at(-s), g), (rm.at[0, o, s, g], rm.at[1, o, s, g]), mate)

    for g in range(subs):
        for o in range(1, ny):
            row_over(o, i, g).start()
    row_mate(i).start()

    half[...] = jnp.zeros_like(half)
    for k in range(blocks):
        at = slice(k * blk, (k + 1) * blk)
        turned = panc[0, :, at].astype(F32).T * pans[k]
        if dp > d:
            turned = jnp.concatenate([turned, jnp.zeros((blk, dp - d), F32)], axis=1)
        first = k * blk
        while first < (k + 1) * blk:
            c = first // bw
            last = min((c + 1) * bw, (k + 1) * blk)
            pg[i, c, first - c * bw : last - c * bw, :] = turned[
                first - k * blk : last - k * blk
            ].astype(BF16)
            first = last

    def turn(n):
        if nhi < 3:
            return n
        if isinstance(n, int):
            return {1: 2, 2: 1}.get(n, n)
        return jnp.where(n == 1, 2, jnp.where(n == 2, 1, n))

    def block_of(n, s):
        return hi_at(turn(n)) * nlo + lo_at(s)

    def pan_mate(q, t, s):
        n = (t - 1) * nlo + (s - 1)
        return send(pg.at[q, block_of(t, s)], (pm.at[0, n], pm.at[1, n]), mate)

    def pan_over(o, q, t, s):
        n = (t - 1) * nlo + (s - 1)
        return send(pg.at[q, block_of(t, s)], (py.at[0, o, n], py.at[1, o, n]), over(o))

    def pan_fwd(o, c, t, s):
        n = (t - 1) * nlo + (s - 1)
        q = chip_at(-o) * 2 + c
        return send(pg.at[q, block_of(t, s)], (pf.at[0, o, n], pf.at[1, o, n]), mate)

    for t in range(1, nhi + 1):
        for s in range(1, nlo + 1):
            for o in range(1, ny):
                pan_over(o, i, t, s).start()
            pan_mate(i, t, s).start()

    def half_of(k):
        both = rowbuf[pl.ds(pl.multiple_of(k * 2 * width, 2 * width), 2 * width), :]

        for p in range(npair):
            got = lax.dot_general(
                amp[p], both, (((1,), (1,)), ((), ())), preferred_element_type=F32
            ).astype(BF16)
            for c in range(2):
                half[k * 2 + c, 0:d, p * width : (p + 1) * width] = got[
                    :, c * width : (c + 1) * width
                ]

    amp_in.wait()
    row_mate(mate_i).wait_recv()
    half_of(chip)

    for g in range(subs + 1):
        for o in range(1, ny):
            if g < subs:
                row_over(o, chip_at(-o) * 2 + core, g).wait_recv()
                for s in range(1, nlo):
                    row_beside(o, s, lo, g).start()
                row_fwd(o, 0, core, g).start()
            if g > 0:
                for s in range(1, nlo):
                    row_beside(o, s, lo_at(-s), g - 1).wait_recv()
                    row_fwd(o, s, core, g - 1).start()

    def half_far(o, carry):
        for s in range(nlo):
            for g in range(subs):
                row_fwd(o, s, 1 - core, g).wait_recv()
        half_of(chip_at(-o))
        return carry

    lax.fori_loop(1, ny, half_far, 0)

    def x_send(t, s, h):
        at = (t - 1, s - 1, h)
        return pltpu.make_async_remote_copy(
            src_ref=xs.at[at], dst_ref=xr.at[at],
            send_sem=xsem.at[(0,) + at], recv_sem=xsem.at[(1,) + at],
            device_id=beside(s), device_id_type=MESH,
        )

    def z_send(t, h):
        at = (t - 1, h)
        return pltpu.make_async_remote_copy(
            src_ref=zs.at[at], dst_ref=zr.at[at],
            send_sem=zsem.at[(0,) + at], recv_sem=zsem.at[(1,) + at],
            device_id=along(turn(t)), device_id_type=MESH,
        )

    def dot(q, b, h):
        return jnp.dot(
            pg[q, b], half[q, :, h * cw : (h + 1) * cw], preferred_element_type=F32
        )

    def partial(b, h):
        acc = dot(i, b, h) + dot(mate_i, b, h)
        for o in range(1, ny):
            for c in range(2):
                acc = acc + dot(chip_at(-o) * 2 + c, b, h)
        return acc

    def added(t, h):
        total = own[t - 1, h]
        for s in range(1, nlo):
            x_send(t, s, h).wait_recv()
            total = total + xr[t - 1, s - 1, h].astype(F32)
        return total

    def pass_on(t):
        for h in range(cuts):
            zs[t - 1, h] = added(t, h).astype(BF16)
            z_send(t, h).start()

    def step(t, carry):
        for s in range(1, nlo + 1):
            b = block_of(t, s)
            for o in range(1, ny):
                q = chip_at(-o) * 2 + core
                pan_over(o, q, t, s).wait_recv()
                pan_fwd(o, core, t, s).start()
            pan_mate(mate_i, t, s).wait_recv()
            for o in range(1, ny):
                pan_fwd(o, 1 - core, t, s).wait_recv()
            for h in range(cuts):
                if s < nlo:
                    xs[t - 1, s - 1, h] = partial(b, h).astype(BF16)
                    x_send(t, s, h).start()
                else:
                    own[t - 1, h] = partial(b, h)

        @pl.when(t > 1)
        def _():
            pass_on(t - 1)

        return carry

    lax.fori_loop(1, nhi + 1, step, 0)

    for h in range(cuts):
        total = added(nhi, h)
        for t in range(1, nhi):
            z_send(t, h).wait_recv()
            total = total + zr[t - 1, h].astype(F32)
        for p in range(cw // width):
            out[:, h * (cw // width) + p, :] = total[:, p * width : (p + 1) * width]

    row_mate(i).wait_send()
    for g in range(subs):
        for o in range(1, ny):
            row_over(o, i, g).wait_send()
            row_fwd(o, 0, core, g).wait_send()
            for s in range(1, nlo):
                row_beside(o, s, lo, g).wait_send()
                row_fwd(o, s, core, g).wait_send()

    def drain(t, carry):
        for s in range(1, nlo + 1):
            pan_mate(i, t, s).wait_send()
            for o in range(1, ny):
                pan_over(o, i, t, s).wait_send()
                pan_fwd(o, core, t, s).wait_send()
            if s < nlo:
                for h in range(cuts):
                    x_send(t, s, h).wait_send()
        return carry

    lax.fori_loop(1, nhi + 1, drain, 0)
    for t in range(1, nhi):
        for h in range(cuts):
            z_send(t, h).wait_send()


def on_device(na, nhi, nlo, row_codes, row_scales, panel_codes, panel_scales, amplitudes):
    npair, d, length = amplitudes.shape
    width = row_codes.shape[1]
    nw = nhi * nlo
    bw = length // nw
    dp = -(-d // 128) * 128
    ny = na // 2
    cols = npair * width
    subs = width // nlo // 16
    by_block = lambda scales: jnp.transpose(scales, (2, 0, 1))
    dma = pltpu.SemaphoreType.DMA
    vmem = pl.BlockSpec(memory_space=pltpu.VMEM)
    return pl.pallas_call(
        functools.partial(kernel, na, nhi, nlo),
        out_shape=jax.ShapeDtypeStruct((bw, npair, width), F32),
        in_specs=[vmem, vmem, vmem, vmem, pl.BlockSpec(memory_space=pl.ANY)],
        out_specs=vmem,
        scratch_shapes=[
            pltpu.VMEM((na * width, length), BF16),
            pltpu.VMEM((na, nw, bw, dp), BF16),
            pltpu.VMEM((na, dp, cols), BF16),
            pltpu.VMEM((npair, d, length), BF16),
            pltpu.VMEM((nhi, 2, bw, cols // 2), F32),
            pltpu.VMEM((nhi, nlo - 1, 2, bw, cols // 2), BF16),
            pltpu.VMEM((nhi, nlo - 1, 2, bw, cols // 2), BF16),
            pltpu.VMEM((nhi - 1, 2, bw, cols // 2), BF16),
            pltpu.VMEM((nhi - 1, 2, bw, cols // 2), BF16),
            dma(()),
            dma((2,)),
            dma((2, ny, subs)),
            dma((2, ny, nlo, subs)),
            dma((2, ny, nlo, subs)),
            dma((2, nw)),
            dma((2, ny, nw)),
            dma((2, ny, nw)),
            dma((2, nhi, nlo - 1, 2)),
            dma((2, nhi - 1, 2)),
        ],
        compiler_params=pltpu.CompilerParams(
            collective_id=0, has_side_effects=True, vmem_limit_bytes=56 * 1024 * 1024
        ),
        cost_estimate=pl.CostEstimate(
            flops=4 * npair * d * length * na * width,
            bytes_accessed=2 * npair * d * length,
            transcendentals=0,
        ),
    )(row_codes, by_block(row_scales), panel_codes, by_block(panel_scales), amplitudes)


def solution(mesh):
    na, nw = mesh.shape["aux"], mesh.shape["virt"]
    nlo = 4 if nw % 16 == 0 else 2
    placed = (
        P("aux", None, None),
        P("aux", None, None),
        P("aux", "virt", None),
        P("aux", "virt", None),
        P("aux", "virt", None),
    )
    return jax.shard_map(
        functools.partial(on_device, na, nw // nlo, nlo),
        mesh=mesh, in_specs=placed, out_specs=P("virt", "aux", None), check_vma=False,
    )
```

time: 60.1 us -> 55.8 us (0.928)
  local copies, waits for them, and re-layouts: 4.72 us -> 1.84 us
  Pallas kernels: 55.1 us -> 53.7 us
    unnamed x3 -> x1, local copies, waits for them, and re-layouts: 4.72 us -> 1.84 us
    pallas_call x1, Pallas kernels: 55.1 us -> 53.7 us  [on_device(): pl.pallas_call(functools.partial(kernel, na, nhi, nlo), out_shape=jax.Sha...]
where the time goes in v2:
time: 55.8 us; the launch traced here: 55.6 us
  Pallas kernels  53.7 us (96%)
  local copies, waits for them, and re-layouts  1.84 us (3%)
    pallas_call x1, Pallas kernels, on_device(): pl.pallas_call(functools.partial(kernel, na, nhi, nlo), out_shape=jax.Sha...  53.7 us
    unnamed x1, local copies, waits for them, and re-layouts  1.84 us

profile of v2, /device:TPU:0, one launch (start us, length us, event | category | flops | bytes accessed | tf_op | source)
XLA Modules:
  0.0 55.6 jit_solution(9098542712190404905)
XLA Ops:
  0.0 53.7 %shard_map.55 = f32[240,4,128]{2,1,0:T(4,128)} custom-call(bf16[1,128,1920]{2,1,0:T(8,128)(2,1)} %rowc.1, f32[15,1,128]{2,1,0:T(1,128)} %bitcast.3, bf16[1,240,1920]{2,1,0:T(8,128)(2,1)} %panc.1, f32[15,1,240]{2,1,0:T(1,128)} %bitcast.2, bf16[4,240,1920]{2,1,0:T(8,128)(2,1)} %amp_hbm.1), custom_call_target="tpu_custom_call" | custom-call | flops 3774873600 | bytes 3686400 | tf_op jit(solution)/shard_map/pallas_call | solution.py:300
  53.7 1.8 %copy.7 = f32[240,4,128]{2,1,0:T(4,128)} copy(f32[240,4,128]{2,1,0:T(4,128)} %shard_map.55) | data formatting | bytes 983040

commit v3 on v2

--- a/solution.py
+++ b/solution.py
@@ -120,15 +120,8 @@
             ].astype(BF16)
             first = last
 
-    def turn(n):
-        if nhi < 3:
-            return n
-        if isinstance(n, int):
-            return {1: 2, 2: 1}.get(n, n)
-        return jnp.where(n == 1, 2, jnp.where(n == 2, 1, n))
-
     def block_of(n, s):
-        return hi_at(turn(n)) * nlo + lo_at(s)
+        return hi_at(n) * nlo + lo_at(s)
 
     def pan_mate(q, t, s):
         n = (t - 1) * nlo + (s - 1)
@@ -199,7 +192,7 @@
         return pltpu.make_async_remote_copy(
             src_ref=zs.at[at], dst_ref=zr.at[at],
             send_sem=zsem.at[(0,) + at], recv_sem=zsem.at[(1,) + at],
-            device_id=along(turn(t)), device_id_type=MESH,
+            device_id=along(t), device_id_type=MESH,
         )
 
     def dot(q, b, h):

time: 55.8 us -> 54.9 us (0.984)
  Pallas kernels: 53.7 us -> 52.9 us
    pallas_call x1, Pallas kernels: 53.7 us -> 52.9 us  [on_device(): pl.pallas_call(functools.partial(kernel, na, nhi, nlo), out_shape=jax.Sha...]
where the time goes in v3:
time: 54.9 us; the launch traced here: 54.7 us
  Pallas kernels  52.9 us (96%)
  local copies, waits for them, and re-layouts  1.84 us (3%)
    pallas_call x1, Pallas kernels, on_device(): pl.pallas_call(functools.partial(kernel, na, nhi, nlo), out_shape=jax.Sha...  52.9 us
    unnamed x1, local copies, waits for them, and re-layouts  1.84 us

profile of v3, /device:TPU:0, one launch (start us, length us, event | category | flops | bytes accessed | tf_op | source)
XLA Modules:
  0.0 54.7 jit_solution(18446632428513664285)
XLA Ops:
  0.0 52.9 %shard_map.55 = f32[240,4,128]{2,1,0:T(4,128)} custom-call(bf16[1,128,1920]{2,1,0:T(8,128)(2,1)} %rowc.1, f32[15,1,128]{2,1,0:T(1,128)} %bitcast.3, bf16[1,240,1920]{2,1,0:T(8,128)(2,1)} %panc.1, f32[15,1,240]{2,1,0:T(1,128)} %bitcast.2, bf16[4,240,1920]{2,1,0:T(8,128)(2,1)} %amp_hbm.1), custom_call_target="tpu_custom_call" | custom-call | flops 3774873600 | bytes 3686400 | tf_op jit(solution)/shard_map/pallas_call | solution.py:293
  52.9 1.8 %copy.7 = f32[240,4,128]{2,1,0:T(4,128)} copy(f32[240,4,128]{2,1,0:T(4,128)} %shard_map.55) | data formatting | bytes 983040
